TPU v7x, 32 devices: a whole 2x2x4 slice. The times are simulated.
32 devices in a mesh: groups: 2 (over y), dp: 4 (over z), tensor: 2 (over x), pipe: 2 (over core).
Axes of the slice: x: 2, y: 2, z: 4, core: 2. Of those that a mesh axis runs over, the one named last changes fastest.
Arguments:
- activations: bfloat16 [8192, 4096], P(('groups', 'dp'), 'tensor'), parts along dimension 0, may hold values from -150 to 150, as said below
- out_grads: bfloat16 [2, 8192, 14336], P('pipe', ('groups', 'dp'), 'tensor'), parts along dimension 1, may hold values from -150 to 150, as said below
- proj_in: bfloat16 [2, 64, 4096], P('pipe', None, 'tensor'), may hold values from -0.09375 to 0.09375
- proj_out: bfloat16 [2, 64, 14336], P('pipe', None, 'tensor'), may hold values from -0.046875 to 0.046875
- sample_ids: int32 [8, 1024], P(('groups', 'dp')), parts along dimension 0, may hold values from 0 to 7, never falling along the last dimension, each value on 1 to 256 neighbouring positions
- queries: bfloat16 [2, 1024, 4096], P('pipe', ('dp', 'tensor')), may hold values from -6 to 6
Outputs:
- scores: float32 [64, 1024], P(('groups', 'dp', 'tensor'), 'pipe'), parts along dimension 0
There are 2 independent parts, one for each index of `groups`. A program takes and returns all parts, laid end to end along the dimension named above; an argument that names none is the same for every part. Nothing has to cross between parts.
Inputs may be any that keep to these rules, and one draw needn't show every extreme that they name: `sample_ids`: each row lists the sample of every token; samples are runs that never fall, every number 0 to 7 appears, each run has 1 to 256 tokens and some run has 256. `activations`: Real-valued. `out_grads`: Real-valued.
All inputs are finite; a program needn't handle non-finite values.
Results may differ from a plain program's by a relative error of at most 0.0078.
Values may be sent and summed in bfloat16 or wider, within the bound.
A program may use at most 128 MiB of HBM per device.

v0:
```python
import jax
import jax.numpy as jnp
from jax import lax
from jax.sharding import PartitionSpec as P

SAMP_DEV = 8


def damped_inverse(factor):
    order_size = factor.shape[0]
    identity = jnp.eye(order_size, dtype=jnp.float32)
    damped = factor + 0.1 * jnp.trace(factor) / order_size * identity
    lower_factor = jnp.linalg.cholesky(damped)
    return jax.scipy.linalg.cho_solve((lower_factor, True), identity)


def body(activations, out_grads, proj_in, proj_out, sample_ids, queries):
    contract = (((1,), (1,)), ((), ()))
    w_out = proj_out[0]
    w_in = proj_in[0]
    part_u = lax.dot_general(w_out, out_grads[0], contract, preferred_element_type=jnp.float32)
    part_v = lax.dot_general(w_in, activations, contract, preferred_element_type=jnp.float32)
    summed = lax.psum(jnp.concatenate([part_u, part_v], 0), "tensor")
    rank_size = w_out.shape[0]
    rounded = summed.astype(jnp.bfloat16)
    u_rows = rounded[:rank_size]
    v_rows = rounded[rank_size:]
    tok_count = u_rows.shape[1]
    total_tokens = tok_count * lax.axis_size("dp")
    out_factor = lax.dot_general(u_rows, u_rows, contract, preferred_element_type=jnp.float32)
    in_factor = lax.dot_general(v_rows, v_rows, contract, preferred_element_type=jnp.float32)
    factors = lax.psum(jnp.concatenate([out_factor, in_factor], 1), "dp")
    factors = factors / total_tokens
    inv_out = damped_inverse(factors[:, :rank_size])
    inv_in = damped_inverse(factors[:, rank_size:])
    per_device = SAMP_DEV // lax.axis_size("tensor")
    own_ids = lax.axis_index("tensor") * per_device + jnp.arange(per_device, dtype=jnp.int32)
    sample_mask = (sample_ids[0][None, :] == own_ids[:, None]).astype(jnp.bfloat16)
    masked = sample_mask[:, None, :] * u_rows[None, :, :]
    sample_grads = jnp.einsum("iat,bt->iab", masked, v_rows, preferred_element_type=jnp.float32)
    precond = jnp.einsum("ac,icb->iab", inv_out, sample_grads, precision=lax.Precision.HIGHEST)
    precond = jnp.einsum("iac,cb->iab", precond, inv_in, precision=lax.Precision.HIGHEST)
    precond = precond.astype(jnp.bfloat16).reshape(per_device, rank_size * rank_size)
    query_rows = queries[0]
    partial_scores = lax.dot_general(
        precond,
        lax.all_gather(query_rows, ("dp", "tensor"), axis=0, tiled=True),
        contract,
        preferred_element_type=jnp.float32,
    )
    return lax.psum_scatter(partial_scores, "pipe", scatter_dimension=1, tiled=True)


def solution(mesh):
    in_specs = (
        P(("groups", "dp"), "tensor"),
        P("pipe", ("groups", "dp"), "tensor"),
        P("pipe", None, "tensor"),
        P("pipe", None, "tensor"),
        P(("groups", "dp"), None),
        P("pipe", ("dp", "tensor"), None),
    )
    out_specs = P(("groups", "dp", "tensor"), "pipe")
    return jax.shard_map(body, mesh=mesh, in_specs=in_specs, out_specs=out_specs, check_vma=False)
```

profile of v0, /device:TPU:1, one launch (start us, length us, event | category | flops | bytes accessed | tf_op | source)
XLA Modules:
  0.0 160.1 jit_solution(17674369221244640815)
XLA Ops:
  6.5 0.0 copy-start
  6.5 0.0 all-gather.3.cloned.1.call-start
  6.5 0.7 all-gather.3.cloned.1.call-update
  7.3 0.0 reduce-scatter.4.cloned.1.call-start
  7.3 3.7 %fusion.10 = f32[64,1024]{1,0:T(8,128)S(1)} fusion(bf16[1024,2048]{1,0:T(8,128)(2,1)} %param.9, bf16[1,64,2048]{2,1,0:T(8,128)(2,1)} %param.11), kind=kOutput, calls=%fused_computation.13 | convolution fusion | flops 268435456 | bytes 4718592 | tf_op jit(solution)/shard_map/dot_general | solution.py:22
  11.0 0.0 copy-done
  11.0 0.0 copy-start.1
  11.0 9.7 %fusion = f32[64,1024]{1,0:T(8,128)S(1)} fusion(bf16[1,1024,7168]{2,1,0:T(8,128)(2,1)} %param.10, bf16[1,64,7168]{2,1,0:T(8,128)(2,1)S(1)} %copy-done), kind=kOutput, calls=%fused_computation | convolution fusion | flops 939524096 | bytes 15859712 | tf_op jit(solution)/shard_map/dot_general | solution.py:21
  20.8 24.0 %all-reduce.1 = bf16[128,1024]{1,0:T(8,128)(2,1)S(1)} all-reduce(f32[128,1024]{1,0:T(8,128)S(1)} %pad_maximum_fusion), channel_id=1, replica_groups=mesh['groups'=2,'dp'=4,'tensor'=2,'pipe'=2] {'tensor'}, use_global_device_ids=true, to_apply=%region_0.0 | all-reduce | flops 131072 | bytes 786432 | tf_op jit(solution)/shard_map/psum | solution.py:23
  44.8 0.2 fusion.15
  45.0 0.2 fusion.30
  45.2 16.7 %psum.15 = f32[64,128]{0,1:T(8,128)S(1)} all-reduce(f32[64,128]{0,1:T(8,128)S(1)} %pad_maximum_fusion.1), channel_id=1, replica_groups=mesh['groups'=2,'dp'=4,'tensor'=2,'pipe'=2] {'dp'}, use_global_device_ids=true, to_apply=%region_1.0 | all-reduce | flops 8192 | bytes 65536 | tf_op jit(solution)/shard_map/psum | solution.py:32
  61.9 0.6 select_reduce_fusion.2
  63.8 0.1 copy.13
  63.8 0.1 copy.14
  63.9 5.8 %cholesky.55 = f32[64,64]{1,0:T(8,128)S(1)} custom-call(f32[64,64]{1,0:T(8,128)S(1)} %get-tuple-element.11), custom_call_target="Cholesky" | custom-call | tf_op jit(solution)/shard_map/jit(cholesky)/cholesky | solution.py:13
  69.8 0.6 compare_reduce_fusion
  70.5 0.7 fusion.23
  71.1 4.9 %custom-call.9 = f32[1,64,64]{1,2,0:T(8,128)S(1)} custom-call(f32[1,64,64]{2,1,0:T(8,128)S(1)} %fusion.23), custom_call_target="InvertDiagBlocksLowerTriangular" | custom-call | tf_op jit(solution)/shard_map/jit(_cho_solve)/triangular_solve | solution.py:14
  76.0 5.9 %cholesky.44 = f32[64,64]{1,0:T(8,128)S(1)} custom-call(f32[64,64]{1,0:T(8,128)S(1)} %get-tuple-element.12), custom_call_target="Cholesky" | custom-call | tf_op jit(solution)/shard_map/jit(cholesky)/cholesky | solution.py:13
  81.9 0.6 compare_reduce_fusion.1
  82.6 0.7 fusion.22
  83.2 4.9 %custom-call.8 = f32[1,64,64]{1,2,0:T(8,128)S(1)} custom-call(f32[1,64,64]{2,1,0:T(8,128)S(1)} %fusion.22), custom_call_target="InvertDiagBlocksLowerTriangular" | custom-call | tf_op jit(solution)/shard_map/jit(_cho_solve)/triangular_solve | solution.py:14
  88.1 0.2 fusion.18
  88.4 0.2 convolution_bitcast_fusion.1
  88.6 0.2 fusion.20
  88.8 0.2 convolution_bitcast_fusion.2
  89.0 0.0 copy-done.1
  89.0 0.1 compare_convert_fusion
  89.0 0.3 fusion.8
  89.3 0.3 convolution_bitcast_fusion
  89.6 0.3 convolution_convert_fusion
  89.9 0.1 reshape.43
  90.0 48.0 %all-gather.3.cloned.1.call-done = bf16[1,1024,4096]{2,1,0:T(8,128)(2,1)} async-done(((bf16[1,128,4096]{2,1,0:T(8,128)(2,1)}), bf16[1,1024,4096]{2,1,0:T(8,128)(2,1)}) %all-gather.3.cloned.1.call-update) | async-done | bytes 8388624 | tf_op jit(solution)/shard_map/all_gather | solution.py:47
  138.0 6.5 %fusion.4 = f32[1024,4]{1,0:T(8,128)} fusion(bf16[4,4096]{1,0:T(4,128)(2,1)S(1)} %reshape.43, bf16[1,1024,4096]{2,1,0:T(8,128)(2,1)} %all-gather.3.cloned.1.call-done), kind=kOutput, calls=%fused_computation.4 | convolution fusion | flops 33554432 | bytes 8437760
  144.5 0.0 reduce-scatter.4.cloned.1.call-update
  144.6 7.1 %reduce-scatter.4.cloned.1.call-done = f32[512,4]{1,0:T(8,128)} async-done(((f32[1024,4]{1,0:T(8,128)}), f32[512,4]{1,0:T(8,128)}) %reduce-scatter.4.cloned.1.call-update) | async-done | bytes 8208
  151.6 1.7 %copy.18 = f32[4,512]{1,0:T(4,128)} copy(f32[4,512]{0,1:T(8,128)} %bitcast.57) | data formatting | bytes 16384
  (9 shorter events, 0.2 us)
Async XLA Ops:
  6.5 4.4 %copy-start = (bf16[1,64,7168]{2,1,0:T(8,128)(2,1)S(1)}, bf16[1,64,7168]{2,1,0:T(8,128)(2,1)}, u32[]{:S(2)}) copy-start(bf16[1,64,7168]{2,1,0:T(8,128)(2,1)} %param.12) | copy-start | bytes 2752516
  6.5 131.5 %all-gather.3.cloned.1.call-start = ((), (), s32[]{:S(2)}) async-start(), calls=%async_computation.1 | async-start | bytes 9437184 | tf_op jit(solution)/shard_map/all_gather | solution.py:47
  7.3 144.4 %reduce-scatter.4.cloned.1.call-start = ((), (), s32[]{:S(2)}) async-start(), calls=%async_computation.2 | async-start | bytes 786432
  11.0 78.0 %copy-start.1 = (s32[1,1024]{1,0:T(1,128)S(1)}, s32[1,1024]{1,0:T(1,128)}, u32[]{:S(2)}) copy-start(s32[1,1024]{1,0:T(1,128)} %param.13) | copy-start | bytes 12292
Sparse Core Ops, SparseCore 0:
  9.5 128.4 all-gather.2
  144.7 6.9 reduce-scatter.3
where the time goes:
time: 161 us; the launch traced here: 160 us
  waiting for transfers between devices  55.8 us (35%)
  blocking collectives  40.7 us (25%)
  other arithmetic  24.9 us (15%)
  matrix products  21.9 us (14%)
  between operations  14.8 us (9%)
  local copies, waits for them, and re-layouts  1.95 us (1%)
    all_gather x1, waiting for transfers between devices, body(): lax.all_gather(query_rows, ('dp', 'tensor'), axis=0, tiled=True)  48 us
    psum x1, blocking collectives, body(): summed = lax.psum(jnp.concatenate([part_u, part_v], 0), 'tensor')  24 us
    psum x1, blocking collectives, body(): factors = lax.psum(jnp.concatenate([out_factor, in_factor], 1), 'dp')  16.7 us
    another operation x6, other arithmetic, damped_inverse(): lower_factor = jnp.linalg.cholesky(damped)  13.1 us
    another operation x4, other arithmetic, damped_inverse(): return jax.scipy.linalg.cho_solve((lower_factor, True), identity)  11.1 us
    dot_general x1, matrix products, body(): lax.dot_general(w_out, out_grads[0], contract, preferred_element_type=jnp...  9.73 us
    unnamed x3, waiting for transfers between devices  7.79 us
    unnamed x1, matrix products  6.53 us
  transfers between devices with their start and end apart: 2, of which 2 were waited for; matrix products, arithmetic and copies ran while one was open for 25% of the time, Pallas kernels for 0%

commit v1 on v0

v1 whole, which is shorter than its diff:
```python
import functools

import jax
import jax.numpy as jnp
from jax import lax
from jax.experimental import pallas as pl
from jax.experimental.pallas import tpu as pltpu
from jax.sharding import PartitionSpec as P

MESH = pl.DeviceIdType.MESH
SAMP_DEV = 8
NT_DIMS = (((1,), (1,)), ((), ()))
NN_DIMS = (((1,), (0,)), ((), ()))
DAMP = 0.1
NEWTON_STEPS = 7


def dot_nt(a, b):
    return lax.dot_general(a, b, NT_DIMS, preferred_element_type=jnp.float32)


def dot_full(a, b):
    return lax.dot_general(
        a, b, NN_DIMS, precision=lax.Precision.HIGHEST, preferred_element_type=jnp.float32
    )


def each(count, step):
    if count <= 16:
        for i in range(count):
            step(i)
    else:
        lax.fori_loop(0, count, lambda i, c: (step(i), c)[1], 0)


def block_diag(packed, low):
    zero = jnp.zeros_like(packed)
    return jnp.concatenate([jnp.where(low, packed, zero), jnp.where(low, zero, packed)], axis=0)


def kernel(
    n_dp, n_t, dims,
    act, og, w_in, w_out, ids, qry, out,
    og_v, act_v, wi_v, wo_v, ids_v, q_v,
    rs_send, rs_recv, own, uv, fac, sg, sg_recv, inv, pre, pre32, s_send, s_recv,
    in_sem, par_sem, rs_ss, rs_rs, f_ss, f_rs, g_ss, g_rs, p_ss, p_rs, o_ss, o_rs,
):
    rank, tok, chunk, per, q_dev = dims
    n = n_dp * n_t
    half = n // 2
    part = tok // n_t
    n_chunk = part // chunk
    my_dp, my_t, my_p = lax.axis_index("dp"), lax.axis_index("tensor"), lax.axis_index("pipe")
    me = my_dp * n_t + my_t

    def at(index, pipe):
        return {"dp": lax.div(index, n_t), "tensor": lax.rem(index, n_t), "pipe": pipe}

    order = [(s, c) for s in list(range(1, n_t)) + [0] for c in range(n_chunk)]

    def chunk_copies(k):
        s, c = order[k]
        start = pl.multiple_of(lax.rem(my_t + s, n_t) * part + c * chunk, chunk)
        rows = pl.ds(start, chunk)
        return (
            pltpu.make_async_copy(og.at[0, rows, :], og_v.at[k], in_sem.at[0, k]),
            pltpu.make_async_copy(act.at[rows, :], act_v.at[k], in_sem.at[1, k]),
        )

    load_wo = pltpu.make_async_copy(w_out.at[0], wo_v, par_sem.at[0])
    load_wi = pltpu.make_async_copy(w_in.at[0], wi_v, par_sem.at[1])
    load_ids = pltpu.make_async_copy(ids, ids_v, par_sem.at[2])
    load_q = pltpu.make_async_copy(qry.at[0], q_v, par_sem.at[3])
    load_wi.start()
    load_wo.start()
    for k in range(len(order)):
        for copy in chunk_copies(k)[::-1]:
            copy.start()
    load_ids.start()
    load_q.start()

    barrier = pltpu.get_barrier_semaphore()

    def greet(k):
        other = lax.rem(me * 2 + my_p + 1 + k, 2 * n)
        pl.semaphore_signal(
            barrier, inc=1, device_id=at(lax.div(other, 2), lax.rem(other, 2)), device_id_type=MESH
        )

    each(2 * n - 1, greet)

    def rs_copy(k):
        s, c = order[k]
        return pltpu.make_async_remote_copy(
            src_ref=rs_send.at[k], dst_ref=rs_recv.at[k],
            send_sem=rs_ss.at[k], recv_sem=rs_rs.at[k],
            device_id={"tensor": lax.rem(my_t + s, n_t)}, device_id_type=MESH,
        )

    n_send = (n_t - 1) * n_chunk
    load_wi.wait()
    load_wo.wait()
    for k, (s, c) in enumerate(order):
        load_og, load_act = chunk_copies(k)
        load_act.wait()
        part_v = dot_nt(wi_v[...], act_v[k])
        load_og.wait()
        part_u = dot_nt(wo_v[...], og_v[k])
        if s > 0:
            rs_send[k, :rank, :] = part_u.astype(jnp.bfloat16)
            rs_send[k, rank:, :] = part_v.astype(jnp.bfloat16)
            if k == 0:
                pl.semaphore_wait(barrier, 2 * n - 1)
            rs_copy(k).start()
        else:
            own[c, :rank, :] = part_u
            own[c, rank:, :] = part_v

    for k in range(n_send):
        rs_copy(k).wait_recv()
    for c in range(n_chunk):
        total = own[c]
        for s in range(1, n_t):
            total = total + rs_recv[(s - 1) * n_chunk + c].astype(jnp.float32)
        uv[:, c * chunk:(c + 1) * chunk] = total.astype(jnp.bfloat16)

    lane = lax.broadcasted_iota(jnp.int32, (rank, 2 * rank), 1)
    row = lax.broadcasted_iota(jnp.int32, (rank, 2 * rank), 0)
    low = lane < rank
    diag = lax.rem(lane, rank) == row
    both = uv[...]
    square = dot_nt(both, both)
    fac[0] = jnp.where(low, square[:rank], square[rank:])

    def f_copy(s):
        return pltpu.make_async_remote_copy(
            src_ref=fac.at[0], dst_ref=fac.at[s], send_sem=f_ss.at[s], recv_sem=f_rs.at[s],
            device_id=at(lax.rem(me + s, n), my_p), device_id_type=MESH,
        )

    each(n - 1, lambda k: f_copy(k + 1).start())

    load_ids.wait()
    own_ids = ids_v[:, pl.ds(pl.multiple_of(my_t * part, 128), part)]
    u_rows, v_rows = uv[:rank, :], uv[rank:, :]

    def g_copy(s):
        return pltpu.make_async_remote_copy(
            src_ref=sg.at[s], dst_ref=sg_recv.at[s - 1], send_sem=g_ss.at[s - 1], recv_sem=g_rs.at[s - 1],
            device_id={"tensor": lax.rem(my_t + s, n_t)}, device_id_type=MESH,
        )

    wide = max(2, per)
    for s in list(range(1, n_t)) + [0]:
        first = lax.rem(my_t + s, n_t) * per
        masked = jnp.concatenate(
            [jnp.where(own_ids == first + i, v_rows.astype(jnp.float32), 0.0) for i in range(wide)], axis=0
        ).astype(jnp.bfloat16)
        sg[s] = dot_nt(u_rows, masked)
        if s > 0:
            g_copy(s).start()

    each(n - 1, lambda k: f_copy(k + 1).wait_recv())
    if n <= 16:
        factor = fac[0]
        for k in range(1, n):
            factor = factor + fac[k]
    else:
        factor = lax.fori_loop(1, n, lambda k, f: f + fac[k], fac[0])
    factor = factor * (1.0 / (tok * n_dp))
    on_diag = jnp.sum(jnp.where(diag, factor, 0.0), axis=0, keepdims=True)
    lane1 = lax.broadcasted_iota(jnp.int32, (1, 2 * rank), 1)
    trace_a = jnp.sum(jnp.where(lane1 < rank, on_diag, 0.0), axis=1, keepdims=True)
    trace_b = jnp.sum(jnp.where(lane1 < rank, 0.0, on_diag), axis=1, keepdims=True)
    trace = jnp.where(lane1 < rank, trace_a, trace_b)
    eye = jnp.where(diag, 1.0, 0.0)
    damped = factor + (DAMP / rank) * trace * eye
    least = (DAMP / rank) / (1.0 + DAMP / rank)
    alpha = 2.0 / (1.0 + least)
    bound = least * alpha
    scale = alpha / ((1.0 + DAMP / rank) * trace)
    state = jnp.concatenate([damped * scale, eye * scale], axis=0)
    for _ in range(NEWTON_STEPS):
        beta = 2.0 / (1.0 + bound * (2.0 - bound))
        bound = beta * bound * (2.0 - bound)
        state = beta * dot_full(state, block_diag(2.0 * eye - state[:rank], low))
    x = state[rank:]
    t = dot_full(damped, block_diag(x, low))
    x = dot_full(x, block_diag(2.0 * eye - t, low))
    inv[...] = x

    for s in range(1, n_t):
        g_copy(s).wait_recv()
    grads = sg[0]
    for s in range(1, n_t):
        grads = grads + sg_recv[s - 1]
    even = inv[pl.ds(0, rank // 2, stride=2), :]
    odd = inv[pl.ds(1, rank // 2, stride=2), :]
    low_half = low[: rank // 2]
    left = jnp.where(low_half, even, pltpu.roll(odd, rank, 1))
    x_in = jnp.where(low, pltpu.roll(x, rank, 1), x)
    right = block_diag(x_in, low)
    blocks = []
    for m in range(wide // 2):
        pair = grads[:, m * 2 * rank:(m + 1) * 2 * rank]
        swapped = pltpu.roll(pair, rank, 1)
        blocks.append(block_diag(jnp.where(low, pair, swapped), low))
        blocks.append(block_diag(jnp.where(low, swapped, pair), low))
    blocks = blocks[:per]
    mid = dot_full(left, jnp.concatenate(blocks, axis=1))
    mid = jnp.concatenate([mid[:, i * 2 * rank:(i + 1) * 2 * rank] for i in range(per)], axis=0)
    pre[me] = dot_full(mid, right).astype(jnp.bfloat16)

    def p_copy(s):
        return pltpu.make_async_remote_copy(
            src_ref=pre.at[me], dst_ref=pre.at[me], send_sem=p_ss.at[s], recv_sem=p_rs.at[s],
            device_id=at(lax.rem(me + s, n), my_p), device_id_type=MESH,
        )

    each(n - 1, lambda k: p_copy(k + 1).start())
    each(n - 1, lambda k: p_copy(k + 1).wait_recv())

    fine = rank // 2
    total_samples = n * per
    pre32[...] = pre[...].astype(jnp.float32).reshape(total_samples * fine, 2 * rank)
    flat = jnp.concatenate(
        [pre32[pl.ds(a, total_samples, stride=fine), :].astype(jnp.bfloat16) for a in range(fine)], axis=1
    )
    load_q.wait()
    scores = dot_nt(flat, q_v[...])
    for j in range(n):
        s_send[j, :per, :q_dev] = scores[j * per:(j + 1) * per]

    my_half = lax.div(me, half)
    slot = my_p * half + lax.rem(me, half)

    def o_copy(s):
        j = lax.rem(me + s, n)
        return pltpu.make_async_remote_copy(
            src_ref=s_send.at[j], dst_ref=s_recv.at[slot], send_sem=o_ss.at[s], recv_sem=o_rs.at[slot],
            device_id=at(j, my_half), device_id_type=MESH,
        )

    each(n - 1, lambda k: o_copy(k + 1).start())

    @pl.when(my_half == my_p)
    def _():
        s_recv[slot] = s_send[me]

    @pl.when(my_half != my_p)
    def _():
        o_copy(0).start()

    def o_wait(k):
        source = my_p * half + lax.rem(k, half)

        @pl.when(jnp.logical_or(source != me, lax.div(k, half) != my_p))
        def _():
            pltpu.make_async_remote_copy(
                src_ref=s_send.at[0], dst_ref=s_recv.at[k], send_sem=o_ss.at[0], recv_sem=o_rs.at[k],
                device_id=at(lax.rem(me + 1, n), my_p), device_id_type=MESH,
            ).wait_recv()

    each(n, o_wait)
    if q_dev % 128 == 0:
        for k in range(half):
            out[:, k * q_dev:(k + 1) * q_dev] = (s_recv[k] + s_recv[half + k])[:per, :q_dev]
    else:
        out[...] = s_recv[:half] + s_recv[half:]

    for k in range(n_send):
        rs_copy(k).wait_send()
    each(n - 1, lambda k: f_copy(k + 1).wait_send())
    for s in range(1, n_t):
        g_copy(s).wait_send()
    each(n - 1, lambda k: p_copy(k + 1).wait_send())
    each(n - 1, lambda k: o_copy(k + 1).wait_send())

    @pl.when(my_half != my_p)
    def _():
        o_copy(0).wait_send()


def body(n_dp, n_t, activations, out_grads, proj_in, proj_out, sample_ids, queries):
    rank = proj_in.shape[1]
    tok, width = activations.shape
    hidden = out_grads.shape[2]
    q_dev, feat = queries.shape[1:]
    n = n_dp * n_t
    half = n // 2
    per = SAMP_DEV // n_t
    part = tok // n_t
    chunk = min(part, 256)
    n_chunk = part // chunk
    n_all, n_send = n_t * n_chunk, (n_t - 1) * n_chunk
    wide = max(2, per) * rank
    lanes = max(q_dev, 128)
    direct = q_dev % 128 == 0
    out_shape = (per, half * q_dev) if direct else (half, 8, lanes)
    bf16, f32 = jnp.bfloat16, jnp.float32
    dma = pltpu.SemaphoreType.DMA
    result = pl.pallas_call(
        functools.partial(kernel, n_dp, n_t, (rank, tok, chunk, per, q_dev)),
        out_shape=jax.ShapeDtypeStruct(out_shape, f32),
        in_specs=[pl.BlockSpec(memory_space=pl.ANY)] * 6,
        out_specs=pl.BlockSpec(memory_space=pltpu.VMEM),
        scratch_shapes=[
            pltpu.VMEM((n_all, chunk, hidden), bf16),
            pltpu.VMEM((n_all, chunk, width), bf16),
            pltpu.VMEM((rank, width), bf16),
            pltpu.VMEM((rank, hidden), bf16),
            pltpu.VMEM(sample_ids.shape, jnp.int32),
            pltpu.VMEM((q_dev, feat), bf16),
            pltpu.VMEM((n_send, 2 * rank, chunk), bf16),
            pltpu.VMEM((n_send, 2 * rank, chunk), bf16),
            pltpu.VMEM((n_chunk, 2 * rank, chunk), f32),
            pltpu.VMEM((2 * rank, part), bf16),
            pltpu.VMEM((n, rank, 2 * rank), f32),
            pltpu.VMEM((n_t, rank, wide), f32),
            pltpu.VMEM((n_t - 1, rank, wide), f32),
            pltpu.VMEM((rank, 2 * rank), f32),
            pltpu.VMEM((n, per * rank // 2, 2 * rank), bf16),
            pltpu.VMEM((n * per * rank // 2, 2 * rank), f32),
            pltpu.VMEM((n, 8, lanes), f32),
            pltpu.VMEM((n, 8, lanes), f32),
            dma((2, n_all)), dma((4,)),
            dma((n_send,)), dma((n_send,)),
            dma((n,)), dma((n,)),
            dma((n_t - 1,)), dma((n_t - 1,)),
            dma((n,)), dma((n,)),
            dma((n,)), dma((n,)),
        ],
        compiler_params=pltpu.CompilerParams(
            collective_id=0, has_side_effects=True, vmem_limit_bytes=56 * 1024 * 1024
        ),
    )(activations, out_grads, proj_in, proj_out, sample_ids, queries)
    if direct:
        return result
    return result[:, :per, :q_dev].transpose(1, 0, 2).reshape(per, half * q_dev)


def solution(mesh):
    in_specs = (
        P(("groups", "dp"), "tensor"),
        P("pipe", ("groups", "dp"), "tensor"),
        P("pipe", None, "tensor"),
        P("pipe", None, "tensor"),
        P(("groups", "dp"), None),
        P("pipe", ("dp", "tensor"), None),
    )
    out_specs = P(("groups", "dp", "tensor"), "pipe")
    return jax.shard_map(
        functools.partial(body, mesh.shape["dp"], mesh.shape["tensor"]),
        mesh=mesh, in_specs=in_specs, out_specs=out_specs, check_vma=False,
    )
```

time: 161 us -> 41.6 us (0.26)
  waiting for transfers between devices: 55.8 us -> 0 us
  blocking collectives: 40.7 us -> 0 us
  Pallas kernels: 0 us -> 40.1 us
  other arithmetic: 24.9 us -> 0 us
  matrix products: 21.9 us -> 0 us
  between operations: 14.8 us -> 0.01 us
    all_gather x1 -> x0, waiting for transfers between devices: 48 us -> none  [body(): lax.all_gather(query_rows, ('dp', 'tensor'), axis=0, tiled=True)]
    psum x2 -> x0, blocking collectives: 40.7 us -> none  [the longest x1 24 us: body(): summed = lax.psum(jnp.concatenate([part_u, part_v], 0), 'tensor')]
    pallas_call x0 -> x1, Pallas kernels: none -> 40.1 us  [body(): pl.pallas_call(functools.partial(kernel, n_dp, n_t, (rank, tok, chunk, pe...]
    another operation x10 -> x0, other arithmetic: 24.2 us -> none  [the longest x6 13.1 us: damped_inverse(): lower_factor = jnp.linalg.cholesky(damped)]
    dot_general x7 -> x0, matrix products: 14.5 us -> none  [the longest x1 9.73 us: body(): lax.dot_general(w_out, out_grads[0], contract, preferred_element_type=jnp...]
    unnamed x3 -> x0, waiting for transfers between devices: 7.79 us -> none
    unnamed x1 -> x0, matrix products: 6.53 us -> none
  transfers between devices with their start and end apart: 2 -> 0, of which waited for: 2 -> 0; matrix products, arithmetic and copies ran while one was open for 25% -> 0% of each run, Pallas kernels for 0% -> 0%
where the time goes in v1:
time: 41.6 us; the launch traced here: 41.4 us
  Pallas kernels  40.1 us (96%)
  local copies, waits for them, and re-layouts  1.3 us (3%)
    pallas_call x1, Pallas kernels, body(): pl.pallas_call(functools.partial(kernel, n_dp, n_t, (rank, tok, chunk, pe...  40.1 us
    unnamed x1, local copies, waits for them, and re-layouts  1.3 us

profile of v1, /device:TPU:1, one launch (start us, length us, event | category | flops | bytes accessed | tf_op | source)
XLA Modules:
  0.0 41.4 jit_solution(2449650779183300531)
XLA Ops:
  0.0 40.1 %shard_map.64 = f32[4,512]{1,0:T(4,128)} custom-call(bf16[1024,2048]{1,0:T(8,128)(2,1)} %act.1, bf16[1,1024,7168]{2,1,0:T(8,128)(2,1)} %og.1, bf16[1,64,2048]{2,1,0:T(8,128)(2,1)} %w_in.1, bf16[1,64,7168]{2,1,0:T(8,128)(2,1)} %w_out.1, s32[1,1024]{1,0:T(1,128)} %ids.1, bf16[1,128,4096]{2,1,0:T(8,128)(2,1)} %qry.1), custom_call_target="tpu_custom_call" | custom-call | tf_op jit(solution)/shard_map/pallas_call | solution.py:302
  40.1 1.3 %copy.8 = f32[4,512]{1,0:T(4,128)} copy(f32[4,512]{1,0:T(4,128)} %shard_map.64) | data formatting | bytes 16384

commit v2 on v1

--- a/solution.py
+++ b/solution.py
@@ -13,10 +13,21 @@
 NN_DIMS = (((1,), (0,)), ((), ()))
 DAMP = 0.1
 NEWTON_STEPS = 7
+PIECES = 1
+CHUNK = 256
+AHEAD = 4
 
 
 def dot_nt(a, b):
     return lax.dot_general(a, b, NT_DIMS, preferred_element_type=jnp.float32)
+
+
+def project(w, x):
+    return dot_nt(x, w)
+
+
+def finish(part):
+    return part.T
 
 
 def dot_full(a, b):
@@ -62,22 +73,30 @@
         s, c = order[k]
         start = pl.multiple_of(lax.rem(my_t + s, n_t) * part + c * chunk, chunk)
         rows = pl.ds(start, chunk)
-        return (
-            pltpu.make_async_copy(og.at[0, rows, :], og_v.at[k], in_sem.at[0, k]),
-            pltpu.make_async_copy(act.at[rows, :], act_v.at[k], in_sem.at[1, k]),
-        )
+        deep = og_v.shape[2] // PIECES
+        cuts = [pl.ds(i * deep, deep) for i in range(PIECES)]
+        return [pltpu.make_async_copy(act.at[rows, :], act_v.at[k], in_sem.at[PIECES, k])] + [
+            pltpu.make_async_copy(og.at[0, rows, cut], og_v.at[k, :, cut], in_sem.at[i, k])
+            for i, cut in enumerate(cuts)
+        ]
 
     load_wo = pltpu.make_async_copy(w_out.at[0], wo_v, par_sem.at[0])
     load_wi = pltpu.make_async_copy(w_in.at[0], wi_v, par_sem.at[1])
     load_ids = pltpu.make_async_copy(ids, ids_v, par_sem.at[2])
     load_q = pltpu.make_async_copy(qry.at[0], q_v, par_sem.at[3])
     load_wi.start()
-    load_wo.start()
-    for k in range(len(order)):
-        for copy in chunk_copies(k)[::-1]:
-            copy.start()
-    load_ids.start()
-    load_q.start()
+    copies = [copy for k in range(len(order)) for copy in chunk_copies(k)]
+    copies = copies[:1] + [load_wo] + copies[1:] + [load_ids, load_q]
+    for copy in copies[:AHEAD]:
+        copy.start()
+    arrived = [0]
+
+    def take():
+        i = arrived[0]
+        copies[i].wait()
+        if i + AHEAD < len(copies):
+            copies[i + AHEAD].start()
+        arrived[0] = i + 1
 
     barrier = pltpu.get_barrier_semaphore()
 
@@ -98,20 +117,29 @@
         )
 
     n_send = (n_t - 1) * n_chunk
+    ready = min(n_send, 2) - 1
     load_wi.wait()
-    load_wo.wait()
     for k, (s, c) in enumerate(order):
-        load_og, load_act = chunk_copies(k)
-        load_act.wait()
-        part_v = dot_nt(wi_v[...], act_v[k])
-        load_og.wait()
-        part_u = dot_nt(wo_v[...], og_v[k])
+        take()
+        part_v = project(wi_v[...], act_v[k])
+        if k == 0:
+            take()
+        part_u = 0.0
+        deep = og_v.shape[2] // PIECES
+        for i in range(PIECES):
+            take()
+            cut = slice(i * deep, (i + 1) * deep)
+            part_u = part_u + project(wo_v[:, cut], og_v[k, :, cut])
+        part_u, part_v = finish(part_u), finish(part_v)
         if s > 0:
             rs_send[k, :rank, :] = part_u.astype(jnp.bfloat16)
             rs_send[k, rank:, :] = part_v.astype(jnp.bfloat16)
-            if k == 0:
+            if k == ready:
                 pl.semaphore_wait(barrier, 2 * n - 1)
-            rs_copy(k).start()
+                for earlier in range(k):
+                    rs_copy(earlier).start()
+            if k >= ready:
+                rs_copy(k).start()
         else:
             own[c, :rank, :] = part_u
             own[c, rank:, :] = part_v
@@ -140,7 +168,7 @@
 
     each(n - 1, lambda k: f_copy(k + 1).start())
 
-    load_ids.wait()
+    take()
     own_ids = ids_v[:, pl.ds(pl.multiple_of(my_t * part, 128), part)]
     u_rows, v_rows = uv[:rank, :], uv[rank:, :]
 
@@ -226,7 +254,7 @@
     flat = jnp.concatenate(
         [pre32[pl.ds(a, total_samples, stride=fine), :].astype(jnp.bfloat16) for a in range(fine)], axis=1
     )
-    load_q.wait()
+    take()
     scores = dot_nt(flat, q_v[...])
     for j in range(n):
         s_send[j, :per, :q_dev] = scores[j * per:(j + 1) * per]
@@ -290,7 +318,7 @@
     half = n // 2
     per = SAMP_DEV // n_t
     part = tok // n_t
-    chunk = min(part, 256)
+    chunk = min(part, CHUNK)
     n_chunk = part // chunk
     n_all, n_send = n_t * n_chunk, (n_t - 1) * n_chunk
     wide = max(2, per) * rank
@@ -323,7 +351,7 @@
             pltpu.VMEM((n * per * rank // 2, 2 * rank), f32),
             pltpu.VMEM((n, 8, lanes), f32),
             pltpu.VMEM((n, 8, lanes), f32),
-            dma((2, n_all)), dma((4,)),
+            dma((PIECES + 1, n_all)), dma((4,)),
             dma((n_send,)), dma((n_send,)),
             dma((n,)), dma((n,)),
             dma((n_t - 1,)), dma((n_t - 1,)),

time: 41.6 us -> 39.7 us (0.954)
  Pallas kernels: 40.1 us -> 38.2 us
    pallas_call x1, Pallas kernels: 40.1 us -> 38.2 us  [body(): pl.pallas_call(functools.partial(kernel, n_dp, n_t, (rank, tok, chunk, pe...]
where the time goes in v2:
time: 39.7 us; the launch traced here: 39.5 us
  Pallas kernels  38.2 us (96%)
  local copies, waits for them, and re-layouts  1.3 us (3%)
    pallas_call x1, Pallas kernels, body(): pl.pallas_call(functools.partial(kernel, n_dp, n_t, (rank, tok, chunk, pe...  38.2 us
    unnamed x1, local copies, waits for them, and re-layouts  1.3 us

profile of v2, /device:TPU:1, one launch (start us, length us, event | category | flops | bytes accessed | tf_op | source)
XLA Modules:
  0.0 39.5 jit_solution(972054209744329394)
XLA Ops:
  0.0 38.2 %shard_map.64 = f32[4,512]{1,0:T(4,128)} custom-call(bf16[1024,2048]{1,0:T(8,128)(2,1)} %act.1, bf16[1,1024,7168]{2,1,0:T(8,128)(2,1)} %og.1, bf16[1,64,2048]{2,1,0:T(8,128)(2,1)} %w_in.1, bf16[1,64,7168]{2,1,0:T(8,128)(2,1)} %w_out.1, s32[1,1024]{1,0:T(1,128)} %ids.1, bf16[1,128,4096]{2,1,0:T(8,128)(2,1)} %qry.1), custom_call_target="tpu_custom_call" | custom-call | tf_op jit(solution)/shard_map/pallas_call | solution.py:330
  38.2 1.3 %copy.8 = f32[4,512]{1,0:T(4,128)} copy(f32[4,512]{1,0:T(4,128)} %shard_map.64) | data formatting | bytes 16384

commit v3 on v2

--- a/solution.py
+++ b/solution.py
@@ -155,10 +155,17 @@
     lane = lax.broadcasted_iota(jnp.int32, (rank, 2 * rank), 1)
     row = lax.broadcasted_iota(jnp.int32, (rank, 2 * rank), 0)
     low = lane < rank
-    diag = lax.rem(lane, rank) == row
+    column = lax.rem(lane, rank)
+    diag = column == row
+    low_half = low[: rank // 2]
     both = uv[...]
     square = dot_nt(both, both)
-    fac[0] = jnp.where(low, square[:rank], square[rank:])
+    packed = jnp.where(low, square[:rank], square[rank:])
+    other = pltpu.roll(packed, rank, 1)
+    mixed = jnp.where(low == (row < column), packed, other)
+    first_diag = jnp.sum(jnp.where(diag, packed, 0.0), axis=0, keepdims=True)
+    fac[0, : rank // 2, :] = jnp.where(low_half, mixed[: rank // 2], mixed[rank // 2:])
+    fac[0, rank // 2:, :] = jnp.broadcast_to(first_diag, (8, 2 * rank))
 
     def f_copy(s):
         return pltpu.make_async_remote_copy(
@@ -195,6 +202,15 @@
             factor = factor + fac[k]
     else:
         factor = lax.fori_loop(1, n, lambda k, f: f + fac[k], fac[0])
+    folded = factor[: rank // 2]
+    turned = pltpu.roll(folded, rank, 1)
+    mixed = jnp.concatenate(
+        [jnp.where(low_half, folded, turned), jnp.where(low_half, turned, folded)], axis=0
+    )
+    mirrored = jnp.concatenate([mixed, mixed], axis=0).T[:rank]
+    first_diag = factor[rank // 2: rank // 2 + 1]
+    factor = jnp.where(low == (row < column), mixed, mirrored)
+    factor = jnp.where(diag, jnp.where(low, first_diag, mixed), factor)
     factor = factor * (1.0 / (tok * n_dp))
     on_diag = jnp.sum(jnp.where(diag, factor, 0.0), axis=0, keepdims=True)
     lane1 = lax.broadcasted_iota(jnp.int32, (1, 2 * rank), 1)
@@ -224,7 +240,6 @@
         grads = grads + sg_recv[s - 1]
     even = inv[pl.ds(0, rank // 2, stride=2), :]
     odd = inv[pl.ds(1, rank // 2, stride=2), :]
-    low_half = low[: rank // 2]
     left = jnp.where(low_half, even, pltpu.roll(odd, rank, 1))
     x_in = jnp.where(low, pltpu.roll(x, rank, 1), x)
     right = block_diag(x_in, low)
@@ -343,7 +358,7 @@
             pltpu.VMEM((n_send, 2 * rank, chunk), bf16),
             pltpu.VMEM((n_chunk, 2 * rank, chunk), f32),
             pltpu.VMEM((2 * rank, part), bf16),
-            pltpu.VMEM((n, rank, 2 * rank), f32),
+            pltpu.VMEM((n, rank // 2 + 8, 2 * rank), f32),
             pltpu.VMEM((n_t, rank, wide), f32),
             pltpu.VMEM((n_t - 1, rank, wide), f32),
             pltpu.VMEM((rank, 2 * rank), f32),

time: 39.7 us -> 38.3 us (0.965)
  Pallas kernels: 38.2 us -> 36.9 us
    pallas_call x1, Pallas kernels: 38.2 us -> 36.9 us  [body(): pl.pallas_call(functools.partial(kernel, n_dp, n_t, (rank, tok, chunk, pe...]
where the time goes in v3:
time: 38.3 us; the launch traced here: 38.2 us
  Pallas kernels  36.9 us (96%)
  local copies, waits for them, and re-layouts  1.3 us (3%)
    pallas_call x1, Pallas kernels, body(): pl.pallas_call(functools.partial(kernel, n_dp, n_t, (rank, tok, chunk, pe...  36.9 us
    unnamed x1, local copies, waits for them, and re-layouts  1.3 us

profile of v3, /device:TPU:1, one launch (start us, length us, event | category | flops | bytes accessed | tf_op | source)
XLA Modules:
  0.0 38.2 jit_solution(17295456541290133772)
XLA Ops:
  0.0 36.9 %shard_map.64 = f32[4,512]{1,0:T(4,128)} custom-call(bf16[1024,2048]{1,0:T(8,128)(2,1)} %act.1, bf16[1,1024,7168]{2,1,0:T(8,128)(2,1)} %og.1, bf16[1,64,2048]{2,1,0:T(8,128)(2,1)} %w_in.1, bf16[1,64,7168]{2,1,0:T(8,128)(2,1)} %w_out.1, s32[1,1024]{1,0:T(1,128)} %ids.1, bf16[1,128,4096]{2,1,0:T(8,128)(2,1)} %qry.1), custom_call_target="tpu_custom_call" | custom-call | tf_op jit(solution)/shard_map/pallas_call | solution.py:345
  36.9 1.3 %copy.8 = f32[4,512]{1,0:T(4,128)} copy(f32[4,512]{1,0:T(4,128)} %shard_map.64) | data formatting | bytes 16384

commit v4 on v3

--- a/solution.py
+++ b/solution.py
@@ -42,6 +42,14 @@
             step(i)
     else:
         lax.fori_loop(0, count, lambda i, c: (step(i), c)[1], 0)
+
+
+def each_partner(n, step):
+    if n <= 16:
+        for s in sorted(range(1, n), key=lambda s: abs(s - n // 2)):
+            step(s)
+    else:
+        lax.fori_loop(1, n, lambda s, c: (step(s), c)[1], 0)
 
 
 def block_diag(packed, low):
@@ -173,7 +181,7 @@
             device_id=at(lax.rem(me + s, n), my_p), device_id_type=MESH,
         )
 
-    each(n - 1, lambda k: f_copy(k + 1).start())
+    each_partner(n, lambda s: f_copy(s).start())
 
     take()
     own_ids = ids_v[:, pl.ds(pl.multiple_of(my_t * part, 128), part)]
@@ -260,7 +268,7 @@
             device_id=at(lax.rem(me + s, n), my_p), device_id_type=MESH,
         )
 
-    each(n - 1, lambda k: p_copy(k + 1).start())
+    each_partner(n, lambda s: p_copy(s).start())
     each(n - 1, lambda k: p_copy(k + 1).wait_recv())
 
     fine = rank // 2
@@ -284,7 +292,7 @@
             device_id=at(j, my_half), device_id_type=MESH,
         )
 
-    each(n - 1, lambda k: o_copy(k + 1).start())
+    each_partner(n, lambda s: o_copy(s).start())
 
     @pl.when(my_half == my_p)
     def _():

time: 38.3 us -> 39.1 us (1.021)
  Pallas kernels: 36.9 us -> 37.6 us
    pallas_call x1, Pallas kernels: 36.9 us -> 37.6 us  [body(): pl.pallas_call(functools.partial(kernel, n_dp, n_t, (rank, tok, chunk, pe...]
where the time goes in v4:
time: 39.1 us; the launch traced here: 38.9 us
  Pallas kernels  37.6 us (96%)
  local copies, waits for them, and re-layouts  1.3 us (3%)
    pallas_call x1, Pallas kernels, body(): pl.pallas_call(functools.partial(kernel, n_dp, n_t, (rank, tok, chunk, pe...  37.6 us
    unnamed x1, local copies, waits for them, and re-layouts  1.3 us

profile of v4, /device:TPU:1, one launch (start us, length us, event | category | flops | bytes accessed | tf_op | source)
XLA Modules:
  0.0 38.9 jit_solution(1726518082773366879)
XLA Ops:
  0.0 37.6 %shard_map.64 = f32[4,512]{1,0:T(4,128)} custom-call(bf16[1024,2048]{1,0:T(8,128)(2,1)} %act.1, bf16[1,1024,7168]{2,1,0:T(8,128)(2,1)} %og.1, bf16[1,64,2048]{2,1,0:T(8,128)(2,1)} %w_in.1, bf16[1,64,7168]{2,1,0:T(8,128)(2,1)} %w_out.1, s32[1,1024]{1,0:T(1,128)} %ids.1, bf16[1,128,4096]{2,1,0:T(8,128)(2,1)} %qry.1), custom_call_target="tpu_custom_call" | custom-call | tf_op jit(solution)/shard_map/pallas_call | solution.py:353
  37.6 1.3 %copy.8 = f32[4,512]{1,0:T(4,128)} copy(f32[4,512]{1,0:T(4,128)} %shard_map.64) | data formatting | bytes 16384
